TPU v7x, 512 devices: a whole 4x4x16 slice. The times are simulated.
512 devices in a mesh: sub: 32 (over z_lo, x, core), freq: 16 (over z_hi, y).
Axes of the slice: x: 4, y: 4, z: 16 (z_hi: 4, z_lo: 4; z = z_hi * 4 + z_lo), core: 2. Of those that a mesh axis runs over, the one named last changes fastest.
Arguments:
- right_side: float32 [16384, 16, 2, 128], P('sub', 'freq'), may hold values from -56 to 56
- schur: bfloat16 [16, 2, 16384, 512], P('freq', None, 'sub'), may hold values from -0.5 to 3.5
- match_blocks: int32 [32, 3], P('sub'), may hold values from 0 to 3
Outputs:
- response: float32 [16, 16384, 128], P('freq', 'sub')
All inputs are finite; a program needn't handle non-finite values.
Results may differ from a plain program's by a relative error of at most 0.0024.
Values may be sent and summed in bfloat16 or wider, within the bound.
A program may use at most 64 MiB of HBM per device.

v0:
```python
import jax
import jax.numpy as jnp
from jax import lax
from jax.sharding import PartitionSpec as P

BLOCK = 128
TIME_DEV = 1
ITERS = 3


KAPPA = 0.5
DECAY = 0.5
EPS = 1e-06


def partner(block, axis, distance):
    count = lax.axis_size(axis)
    route = []
    for low in range(count):
        high = low | 1 << distance
        if high != low and high < count:
            route += [(low, high), (high, low)]
    return lax.ppermute(block, axis, route)


def phase_table(times, freqs, total_times, total_freqs):
    level = (2 * freqs[None, :] + 1) * times[:, None] % (2 * total_times)
    angle = jnp.pi * level.astype(jnp.float32) / total_times
    damp = jnp.exp(DECAY * times.astype(jnp.float32) / total_times) / jnp.sqrt(
        jnp.float32(total_freqs)
    )
    return jnp.stack([jnp.cos(angle), -jnp.sin(angle)], axis=2) * damp[:, None, None]


def shards(right_side, schur, match_blocks):
    nsub = lax.axis_size("sub")
    logs = nsub.bit_length() - 1
    nfreq = lax.axis_size("freq")
    ni = right_side.shape[0]
    fdev = right_side.shape[1]
    loads = right_side.shape[3]
    rounds = match_blocks.shape[1]
    own_blocks = match_blocks[0]
    high = lax.Precision.HIGHEST
    sequence = list(range(rounds))
    res = right_side
    sol_re = jnp.zeros(res[:, :, 0].shape, jnp.float32)
    sol_im = jnp.zeros(res[:, :, 0].shape, jnp.float32)
    for step in range(ITERS):
        q = res.astype(jnp.bfloat16)
        flat = q.reshape(ni, fdev, 2 * loads)
        prod = jnp.einsum("fcij,jfk->ifck", schur, flat, preferred_element_type=jnp.float32)
        real = prod[:, :, 0, :loads] - prod[:, :, 1, loads:]
        imag = prod[:, :, 0, loads:] + prod[:, :, 1, :loads]
        total = jnp.stack([real, imag], axis=2)
        couple = jnp.zeros(total.shape, jnp.float32)
        for rnd in sequence:
            bit = rnd * logs // rounds
            start = own_blocks[rnd] * BLOCK
            outgoing = lax.dynamic_slice_in_dim(q, start, BLOCK, 0)
            incoming = partner(outgoing, "sub", bit)
            current = lax.dynamic_slice_in_dim(couple, start, BLOCK, 0)
            couple = lax.dynamic_update_slice_in_dim(
                couple, current + incoming.astype(jnp.float32), start, 0
            )
        image = total - KAPPA * couple
        w_re, w_im = (image[:, :, 0], image[:, :, 1])
        r_re, r_im = (res[:, :, 0], res[:, :, 1])
        part_re = jnp.sum(w_re * r_re + w_im * r_im, axis=0)
        part_im = jnp.sum(w_re * r_im - w_im * r_re, axis=0)
        part_den = jnp.sum(w_re * w_re + w_im * w_im, axis=0)
        num_re, num_im, den = lax.psum((part_re, part_im, part_den), "sub")
        den = den + EPS
        a_re = num_re / den
        a_im = num_im / den
        sol_re = sol_re + a_re * r_re - a_im * r_im
        sol_im = sol_im + a_re * r_im + a_im * r_re
        new_re = r_re - (a_re * w_re - a_im * w_im)
        new_im = r_im - (a_re * w_im + a_im * w_re)
        res = jnp.stack([new_re, new_im], axis=2)
    solution = jnp.stack([sol_re, sol_im], axis=2)
    freqs_total = fdev * nfreq
    times_total = TIME_DEV * nfreq
    first_freq = lax.axis_index("freq") * fdev
    times = jnp.arange(TIME_DEV * lax.axis_size("freq"), dtype=jnp.int32)
    freqs = first_freq + jnp.arange(fdev, dtype=jnp.int32)
    table = phase_table(times, freqs, times_total, freqs_total)
    return lax.psum_scatter(
        jnp.einsum("kfc,ifcl->kil", table, solution, precision=high),
        "freq",
        scatter_dimension=0,
        tiled=True,
    )


def solution(mesh):
    return jax.shard_map(
        shards,
        mesh=mesh,
        in_specs=(P("sub", "freq", None, None), P("freq", None, "sub", None), P("sub", None)),
        out_specs=P("freq", "sub", None),
        check_vma=False,
    )
```

profile of v0, /device:TPU:1, one launch (start us, length us, event | category | flops | bytes accessed | tf_op | source)
XLA Modules:
  0.0 423.8 jit_solution(4717913310621227963)
XLA Ops:
  6.5 0.0 copy-start
  6.5 0.0 reduce-scatter.2.cloned.1.call-start
  6.5 1.4 fusion.43
  9.9 1.2 copy.9
  11.3 4.4 %collective-permute-start.2 = (bf16[128,1,2,128]{0,3,2,1:T(8,128)(2,1)S(1)}, bf16[128,1,2,128]{0,3,2,1:T(8,128)(2,1)S(1)}, u32[]{:S(2)}, u32[]{:S(2)}) collective-permute-start(bf16[128,1,2,128]{0,3,2,1:T(8,128)(2,1)S(1)} %get-tuple-element.53), channel_id=1, source_target_pairs={{0,128},{128,0},{16,144},{144,16},{32,160},{160,32},{48,176},{176,... | collective-permute-start | bytes 196616 | tf_op jit(solution)/shard_map/ppermute | solution.py:23
  15.7 3.1 collective-permute-start.1
  18.8 5.1 %collective-permute-start = (bf16[128,1,2,128]{0,3,2,1:T(8,128)(2,1)S(1)}, bf16[128,1,2,128]{0,3,2,1:T(8,128)(2,1)S(1)}, u32[]{:S(2)}, u32[]{:S(2)}) collective-permute-start(bf16[128,1,2,128]{0,3,2,1:T(8,128)(2,1)S(1)} %get-tuple-element.55), channel_id=1, source_target_pairs={{0,16},{16,0},{32,48},{48,32},{64,80},{80,64},{96,112},{112,96},{1... | collective-permute-start | bytes 196616 | tf_op jit(solution)/shard_map/ppermute | solution.py:23
  23.9 0.1 negate_bitcast_fusion
  24.0 0.0 copy-done
  24.0 0.5 convolution_bitcast_fusion.2
  24.5 0.1 slice_subtract_fusion.2
  24.6 0.2 collective-permute-done
  24.9 0.0 collective-permute-done.1
  24.9 0.0 collective-permute-done.2
  25.0 0.1 maximum_subtract_fusion
  25.1 0.2 fusion.14
  25.3 68.1 %all-reduce.2 = (f32[1,128]{1,0:T(1,128)S(1)}, f32[1,128]{1,0:T(1,128)S(1)}, f32[1,128]{1,0:T(1,128)S(1)}) all-reduce(f32[1,128]{1,0:T(1,128)S(1)} %bitcast.188, f32[1,128]{1,0:T(1,128)S(1)} %bitcast.189, f32[1,128]{1,0:T(1,128)S(1)} %bitcast.187), channel_id=1, replica_groups=mesh['sub'=32,'freq'=16] {'sub'}, use_global_device_ids=true, to_apply=%region_5.0 | all-reduce | flops 384 | bytes 3072 | tf_op jit(solution)/shard_map/psum | solution.py:72
  93.3 0.2 fusion.42
  93.6 1.9 collective-permute-start.5
  95.5 3.8 collective-permute-start.3
  99.3 1.9 collective-permute-start.4
  101.3 0.5 convolution_bitcast_fusion.1
  101.7 0.1 slice_subtract_fusion.1
  101.8 0.0 collective-permute-done.3
  101.8 0.1 broadcast.801.clone.1
  101.9 3.0 collective-permute-done.4
  105.0 0.0 collective-permute-done.5
  105.0 0.1 maximum_subtract_fusion.1
  105.1 1.0 fusion.4
  106.1 67.5 %all-reduce.1 = (f32[1,128]{1,0:T(1,128)S(1)}, f32[1,128]{1,0:T(1,128)S(1)}, f32[1,128]{1,0:T(1,128)S(1)}) all-reduce(f32[1,128]{1,0:T(1,128)S(1)} %bitcast.191, f32[1,128]{1,0:T(1,128)S(1)} %bitcast.192, f32[1,128]{1,0:T(1,128)S(1)} %bitcast.190), channel_id=1, replica_groups=mesh['sub'=32,'freq'=16] {'sub'}, use_global_device_ids=true, to_apply=%region_11.0 | all-reduce | flops 384 | bytes 3072 | tf_op jit(solution)/shard_map/psum | solution.py:72
  173.6 0.0 copy-start.1
  173.6 0.0 copy-start.2
  173.7 0.2 fusion.39
  173.9 1.9 collective-permute-start.8
  175.8 2.8 collective-permute-start.6
  178.6 1.9 collective-permute-start.7
  180.5 0.5 convolution_bitcast_fusion
  181.0 0.0 copy-done.1
  181.0 0.0 copy-done.2
  181.0 0.1 fusion.10
  181.2 0.1 slice_subtract_fusion
  181.3 0.0 collective-permute-done.6
  181.3 0.1 broadcast.801
  181.3 2.9 collective-permute-done.7
  184.2 0.0 collective-permute-done.8
  184.3 0.1 maximum_subtract_fusion.2
  184.4 0.2 add_reduce_fusion.1
  184.6 67.5 %all-reduce = (f32[1,128]{1,0:T(1,128)S(1)}, f32[1,128]{1,0:T(1,128)S(1)}, f32[1,128]{1,0:T(1,128)S(1)}) all-reduce(f32[1,128]{1,0:T(1,128)S(1)} %bitcast.185, f32[1,128]{1,0:T(1,128)S(1)} %bitcast.186, f32[1,128]{1,0:T(1,128)S(1)} %bitcast.184), channel_id=1, replica_groups=mesh['sub'=32,'freq'=16] {'sub'}, use_global_device_ids=true, to_apply=%region_17.0 | all-reduce | flops 384 | bytes 3072 | tf_op jit(solution)/shard_map/psum | solution.py:72
  252.1 0.3 multiply_subtract_fusion
  252.5 0.2 copy.12
  252.7 3.5 fusion.29
  256.3 3.2 copy.13
  259.5 0.0 reduce-scatter.2.cloned.1.call-update
  259.5 157.4 %reduce-scatter.2.cloned.1.call-done = f32[1,512,128]{2,1,0:T(8,128)} async-done(((f32[16,512,128]{2,1,0:T(8,128)}), f32[1,512,128]{2,1,0:T(8,128)}) %reduce-scatter.2.cloned.1.call-update) | async-done | bytes 262160 | tf_op jit(solution)/shard_map/reduce_scatter | solution.py:88
  (21 shorter events, 0.6 us)
Async XLA Ops:
  6.5 17.4 %copy-start = (bf16[1,2,512,512]{3,2,1,0:T(8,128)(2,1)S(1)}, bf16[1,2,512,512]{3,2,1,0:T(8,128)(2,1)}, u32[]{:S(2)}) copy-start(bf16[1,2,512,512]{3,2,1,0:T(8,128)(2,1)} %param.4) | copy-start | bytes 3145732
  6.5 410.4 %reduce-scatter.2.cloned.1.call-start = ((), (), s32[]{:S(2)}) async-start(), calls=%async_computation.1 | async-start | bytes 4456448 | tf_op jit(solution)/shard_map/reduce_scatter | solution.py:88
  11.3 13.7 %collective-permute-start.2 = (bf16[128,1,2,128]{0,3,2,1:T(8,128)(2,1)S(1)}, bf16[128,1,2,128]{0,3,2,1:T(8,128)(2,1)S(1)}, u32[]{:S(2)}, u32[]{:S(2)}) collective-permute-start(bf16[128,1,2,128]{0,3,2,1:T(8,128)(2,1)S(1)} %get-tuple-element.53), channel_id=1, source_target_pairs={{0,128},{128,0},{16,144},{144,16},{32,160},{160,32},{48,176},{176,... | collective-permute-start | bytes 196616 | tf_op jit(solution)/shard_map/ppermute | solution.py:23
  15.7 9.2 %collective-permute-start.1 = (bf16[128,1,2,128]{0,3,2,1:T(8,128)(2,1)S(1)}, bf16[128,1,2,128]{0,3,2,1:T(8,128)(2,1)S(1)}, u32[]{:S(2)}, u32[]{:S(2)}) collective-permute-start(bf16[128,1,2,128]{0,3,2,1:T(8,128)(2,1)S(1)} %get-tuple-element.54), channel_id=1, source_target_pairs={{0,32},{32,0},{16,48},{48,16},{64,96},{96,64},{80,112},{112,80},{1... | collective-permute-start | bytes 196616 | tf_op jit(solution)/shard_map/ppermute | solution.py:23
  18.8 6.0 %collective-permute-start = (bf16[128,1,2,128]{0,3,2,1:T(8,128)(2,1)S(1)}, bf16[128,1,2,128]{0,3,2,1:T(8,128)(2,1)S(1)}, u32[]{:S(2)}, u32[]{:S(2)}) collective-permute-start(bf16[128,1,2,128]{0,3,2,1:T(8,128)(2,1)S(1)} %get-tuple-element.55), channel_id=1, source_target_pairs={{0,16},{16,0},{32,48},{48,32},{64,80},{80,64},{96,112},{112,96},{1... | collective-permute-start | bytes 196616 | tf_op jit(solution)/shard_map/ppermute | solution.py:23
  93.6 11.4 %collective-permute-start.5 = (bf16[128,1,2,128]{0,3,2,1:T(8,128)(2,1)S(1)}, bf16[128,1,2,128]{0,3,2,1:T(8,128)(2,1)S(1)}, u32[]{:S(2)}, u32[]{:S(2)}) collective-permute-start(bf16[128,1,2,128]{0,3,2,1:T(8,128)(2,1)S(1)} %get-tuple-element.50), channel_id=1, source_target_pairs={{0,128},{128,0},{16,144},{144,16},{32,160},{160,32},{48,176},{176,... | collective-permute-start | bytes 196616 | tf_op jit(solution)/shard_map/ppermute | solution.py:23
  95.5 6.3 %collective-permute-start.3 = (bf16[128,1,2,128]{0,3,2,1:T(8,128)(2,1)S(1)}, bf16[128,1,2,128]{0,3,2,1:T(8,128)(2,1)S(1)}, u32[]{:S(2)}, u32[]{:S(2)}) collective-permute-start(bf16[128,1,2,128]{0,3,2,1:T(8,128)(2,1)S(1)} %get-tuple-element.51), channel_id=1, source_target_pairs={{0,16},{16,0},{32,48},{48,32},{64,80},{80,64},{96,112},{112,96},{1... | collective-permute-start | bytes 196616 | tf_op jit(solution)/shard_map/ppermute | solution.py:23
  99.3 5.6 %collective-permute-start.4 = (bf16[128,1,2,128]{0,3,2,1:T(8,128)(2,1)S(1)}, bf16[128,1,2,128]{0,3,2,1:T(8,128)(2,1)S(1)}, u32[]{:S(2)}, u32[]{:S(2)}) collective-permute-start(bf16[128,1,2,128]{0,3,2,1:T(8,128)(2,1)S(1)} %get-tuple-element.52), channel_id=1, source_target_pairs={{0,32},{32,0},{16,48},{48,16},{64,96},{96,64},{80,112},{112,80},{1... | collective-permute-start | bytes 196616 | tf_op jit(solution)/shard_map/ppermute | solution.py:23
  173.6 7.4 %copy-start.1 = (f32[512,1,128]{0,2,1:T(8,128)S(1)}, f32[512,1,128]{0,2,1:T(8,128)}, u32[]{:S(2)}) copy-start(f32[512,1,128]{0,2,1:T(8,128)} %get-tuple-element.27) | copy-start | bytes 786436
  173.6 7.4 %copy-start.2 = (f32[512,1,128]{0,2,1:T(8,128)S(1)}, f32[512,1,128]{0,2,1:T(8,128)}, u32[]{:S(2)}) copy-start(f32[512,1,128]{0,2,1:T(8,128)} %get-tuple-element.28) | copy-start | bytes 786436
  173.9 10.3 %collective-permute-start.8 = (bf16[128,1,2,128]{0,3,2,1:T(8,128)(2,1)S(1)}, bf16[128,1,2,128]{0,3,2,1:T(8,128)(2,1)S(1)}, u32[]{:S(2)}, u32[]{:S(2)}) collective-permute-start(bf16[128,1,2,128]{0,3,2,1:T(8,128)(2,1)S(1)} %get-tuple-element.47), channel_id=1, source_target_pairs={{0,128},{128,0},{16,144},{144,16},{32,160},{160,32},{48,176},{176,... | collective-permute-start | bytes 196616 | tf_op jit(solution)/shard_map/ppermute | solution.py:23
  175.8 5.4 %collective-permute-start.6 = (bf16[128,1,2,128]{0,3,2,1:T(8,128)(2,1)S(1)}, bf16[128,1,2,128]{0,3,2,1:T(8,128)(2,1)S(1)}, u32[]{:S(2)}, u32[]{:S(2)}) collective-permute-start(bf16[128,1,2,128]{0,3,2,1:T(8,128)(2,1)S(1)} %get-tuple-element.48), channel_id=1, source_target_pairs={{0,16},{16,0},{32,48},{48,32},{64,80},{80,64},{96,112},{112,96},{1... | collective-permute-start | bytes 196616 | tf_op jit(solution)/shard_map/ppermute | solution.py:23
  178.6 5.6 %collective-permute-start.7 = (bf16[128,1,2,128]{0,3,2,1:T(8,128)(2,1)S(1)}, bf16[128,1,2,128]{0,3,2,1:T(8,128)(2,1)S(1)}, u32[]{:S(2)}, u32[]{:S(2)}) collective-permute-start(bf16[128,1,2,128]{0,3,2,1:T(8,128)(2,1)S(1)} %get-tuple-element.49), channel_id=1, source_target_pairs={{0,32},{32,0},{16,48},{48,16},{64,96},{96,64},{80,112},{112,80},{1... | collective-permute-start | bytes 196616 | tf_op jit(solution)/shard_map/ppermute | solution.py:23
Sparse Core Ops, SparseCore 0:
  259.6 157.2 reduce-scatter.1
where the time goes:
time: 424 us
  blocking collectives  203 us (48%)
  waiting for transfers between devices  164 us (39%)
  starting transfers between devices  26.9 us (6%)
  between operations  15.8 us (4%)
  local copies, waits for them, and re-layouts  6.27 us (1%)
  matrix products  4.94 us (1%)
    psum x3, blocking collectives, shards(): num_re, num_im, den = lax.psum((part_re, part_im, part_den), 'sub')  203 us
    reduce_scatter x1, waiting for transfers between devices, shards(): lax.psum_scatter(jnp.einsum('kfc,ifcl->kil', table, solution, precision=h...  157 us
    ppermute x9, starting transfers between devices, partner(): return lax.ppermute(block, axis, route)  26.9 us
  transfers between devices with their start and end apart: 10, of which 4 were waited for; matrix products, arithmetic and copies ran while one was open for 1% of the time, Pallas kernels for 0%

commit v1 on v0

v1 whole, which is shorter than its diff:
```python
import jax
import jax.numpy as jnp
import numpy as np
from jax import lax
from jax.experimental import pallas as pl
from jax.experimental.pallas import tpu as pltpu
from jax.sharding import PartitionSpec as P

MESH = pl.DeviceIdType.MESH
F32 = jnp.float32
BF16 = jnp.bfloat16

BLOCK = 128
KAPPA = 0.5
DECAY = 0.5
EPS = 1e-06
ROUNDS = 3
NY = 4
CH = 32


def phase_table(count):
    times = np.arange(count)
    freqs = np.arange(count)
    level = (2 * freqs[None, :] + 1) * times[:, None] % (2 * count)
    angle = np.pi * level / count
    damp = np.exp(DECAY * times / count) / np.sqrt(count)
    table = np.stack([np.cos(angle), -np.sin(angle)], axis=2) * damp[:, None, None]
    return table.astype(np.float32).reshape(-1)


def cmul(a, b):
    return (a[0] * b[0] - a[1] * b[1], a[0] * b[1] + a[1] * b[0])


def conj(a):
    return (a[0], -a[1])


def cadd(a, b):
    return (a[0] + b[0], a[1] + b[1])


def csub(a, b):
    return (a[0] - b[0], a[1] - b[1])


def scale(r, a):
    return (r * a[0], r * a[1])


def abs2(a):
    return a[0] * a[0] + a[1] * a[1]


def divide(a, d):
    return (a[0] / d, a[1] / d)


def combination(g):
    g10, g11, g20, g21, g22, g30, g31, g32, g33 = g
    a0 = divide(g10, g11 + EPS)
    n1 = csub(g10, scale(g11, a0))
    n1 = csub(n1, cmul(conj(a0), g20))
    n1 = cadd(n1, scale(abs2(a0), g21))
    d1 = g11 - 2.0 * cmul(a0, conj(g21))[0] + abs2(a0) * g22
    a1 = divide(n1, jnp.maximum(d1, 0.0) + EPS)
    b = cadd(a0, a1)
    d = cmul(a0, a1)
    n2 = cadd(csub(g10, scale(g11, b)), cmul(d, conj(g21)))
    t = cadd(csub(g20, cmul(b, g21)), scale(g22, d))
    n2 = csub(n2, cmul(conj(b), t))
    t = cadd(csub(g30, cmul(b, g31)), cmul(d, g32))
    n2 = cadd(n2, cmul(conj(d), t))
    d2 = g11 + abs2(b) * g22 + abs2(d) * g33
    d2 = d2 - 2.0 * cmul(b, conj(g21))[0] + 2.0 * cmul(d, conj(g31))[0]
    d2 = d2 - 2.0 * cmul(cmul(conj(b), d), conj(g32))[0]
    a2 = divide(n2, jnp.maximum(d2, 0.0) + EPS)
    w0 = cadd(b, a2)
    w1 = scale(-1.0, cadd(d, cmul(a2, b)))
    wu = scale(-1.0, cmul(a2, a1))
    w2 = cmul(d, a2)
    return w0, w1, wu, w2


def kernel(
    mb_hbm, tbl_hbm, rs_hbm, sch_hbm, out_ref,
    mb, tbl, rs, sch, v0, v1, v2, u1, q, qlo, prod,
    ex_send, ex_recv, ga_send, ga_recv, gb_send, gb_recv,
    z1s, z1r, y1s, y1r, own, p2s, p2r, keep, z3s, z3r, y3s, y3r,
    in_sem, ex_ss, ex_rs, ga_ss, ga_rs, gb_ss, gb_rs,
    z1_ss, z1_rs, y1_ss, y1_rs, p2_ss, p2_rs, z3_ss, z3_rs, y3_ss, y3_rs,
):
    s = lax.axis_index("sub")
    f = lax.axis_index("freq")
    nsub = lax.axis_size("sub")
    z, y = f // NY, f % NY
    ni = v0.shape[0]
    nb = ni // BLOCK
    load = v0.shape[1] // 2

    def flip(bit):
        return s + bit - 2 * bit * ((s // bit) % 2)

    partners = [flip(1), flip(2), flip(8)]
    group = [(s // 8) * 8 + (s + off) % 8 for off in range(1, 8)]
    layers = [(s + 8 * off) % nsub for off in range(1, 4)]
    ze = z + 1 - 2 * (z % 2)
    zo = 3 - z
    opp = 3 - ze
    za = (ze, zo)

    def yt(off):
        return (y + off) % NY

    def yf(off):
        return (y + NY - off) % NY

    sends = []

    def send(src, dst, ss, rsem, sub, freq):
        copy = pltpu.make_async_remote_copy(
            src_ref=src, dst_ref=dst, send_sem=ss, recv_sem=rsem,
            device_id={"sub": sub, "freq": freq}, device_id_type=MESH,
        )
        copy.start()
        sends.append(copy)
        return copy

    c_mb = pltpu.make_async_copy(mb_hbm, mb, in_sem.at[0])
    c_tbl = pltpu.make_async_copy(tbl_hbm, tbl, in_sem.at[1])
    c_rs = pltpu.make_async_copy(rs_hbm, rs, in_sem.at[2])
    c_sch = pltpu.make_async_copy(sch_hbm, sch, in_sem.at[3])
    c_rs.start()
    c_mb.start()
    c_sch.start()
    c_tbl.start()

    barrier = pltpu.get_barrier_semaphore()
    peers = [(p, f) for p in group + layers]
    peers += [(s, z * NY + yt(off)) for off in range(1, NY)]
    peers += [(s, zt * NY + yt(off)) for zt in za for off in range(NY)]
    for ps, pf in peers:
        pl.semaphore_signal(barrier, inc=1, device_id={"sub": ps, "freq": pf}, device_id_type=MESH)

    c_rs.wait()
    for k in range(nb):
        for c in range(2):
            part = rs[pl.ds(2 * BLOCK * k + c, BLOCK, stride=2), :]
            rows, cols = pl.ds(k * BLOCK, BLOCK), pl.ds(c * load, load)
            v0[rows, cols] = part
            high = part.astype(BF16)
            q[rows, cols] = high
            qlo[rows, cols] = (part - high.astype(F32)).astype(BF16)
    c_mb.wait()
    pl.semaphore_wait(barrier, len(peers))

    def match(r, k):
        gap = (mb[0, r] - k).astype(F32)
        return jnp.maximum(1.0 - gap * gap, 0.0)

    def exchange(j):
        out = []
        for r in (1, 2, 0):
            block = None
            for k in range(nb):
                part = match(r, k) * q[pl.ds(k * BLOCK, BLOCK), :].astype(F32)
                block = part if block is None else block + part
            ex_send[j, r] = block.astype(BF16)
            out.append(send(ex_send.at[j, r], ex_recv.at[j, r], ex_ss.at[j, r], ex_rs.at[j, r], partners[r], f))
        return out

    def image(j, k):
        top = prod[pl.ds(k * BLOCK, BLOCK), :]
        low = prod[pl.ds(ni + k * BLOCK, BLOCK), :]
        re = top[:, :load] - low[:, load:]
        im = top[:, load:] + low[:, :load]
        if j is not None:
            for r in range(ROUNDS):
                weight = KAPPA * match(r, k)
                inc = ex_recv[j, r].astype(F32)
                re = re - weight * inc[:, :load]
                im = im - weight * inc[:, load:]
        return re, im

    def fold(a):
        return jnp.sum(a.reshape(BLOCK // 8, 8, load), axis=0)

    def pair(v, k):
        rows = pl.ds(k * BLOCK, BLOCK)
        return v[rows, :load], v[rows, load:]

    def inner(a, b):
        return [fold(a[0] * b[0] + a[1] * b[1]), fold(a[0] * b[1] - a[1] * b[0])]

    def total(parts):
        acc = parts[0]
        for p in parts[1:]:
            acc = [i + j for i, j in zip(acc, p)]
        return [jnp.sum(a, axis=0, keepdims=True) for a in acc]

    moves = exchange(0)
    c_sch.wait()
    prod[...] = jnp.dot(sch[...], qlo[...], preferred_element_type=F32)
    for k in range(nb):
        re, im = image(None, k)
        rows = pl.ds(k * BLOCK, BLOCK)
        u1[rows, :load] = re
        u1[rows, load:] = im
    prod[...] = jnp.dot(sch[...], q[...], preferred_element_type=F32)
    for m in moves:
        m.wait_recv()
    for k in range(nb):
        re, im = image(0, k)
        rows = pl.ds(k * BLOCK, BLOCK)
        v1[rows, :load] = re
        v1[rows, load:] = im
        q[rows, :load] = re.astype(BF16)
        q[rows, load:] = im.astype(BF16)
    moves = exchange(1)
    for k in range(nb):
        rows = pl.ds(k * BLOCK, BLOCK)
        qlo[rows, :] = (v1[rows, :] - q[rows, :].astype(F32)).astype(BF16)
    prod[...] = jnp.dot(sch[...], q[...], preferred_element_type=F32) + jnp.dot(
        sch[...], qlo[...], preferred_element_type=F32
    )
    rows1 = []
    for k in range(nb):
        a = pair(v1, k)
        rows1.append(inner(a, pair(v0, k)) + [fold(abs2(a))])
    rows1 = total(rows1)
    for m in moves:
        m.wait_recv()
    for k in range(nb):
        re, im = image(1, k)
        rows = pl.ds(k * BLOCK, BLOCK)
        v2[rows, :load] = re
        v2[rows, load:] = im
        q[rows, :load] = re.astype(BF16)
        q[rows, load:] = im.astype(BF16)
    moves = exchange(2)
    prod[...] = jnp.dot(sch[...], q[...], preferred_element_type=F32)
    rows2 = []
    for k in range(nb):
        a = pair(v2, k)
        rows2.append(inner(a, pair(v0, k)) + inner(a, pair(v1, k)) + [fold(abs2(a))])
    rows2 = total(rows2)
    for m in moves:
        m.wait_recv()
    rows3 = []
    for k in range(nb):
        a = image(2, k)
        rows3.append(
            inner(a, pair(v0, k)) + inner(a, pair(v1, k)) + inner(a, pair(v2, k)) + [fold(abs2(a))]
        )
    rows3 = total(rows3)

    for i, row in enumerate(rows1 + rows2 + rows3):
        ga_send[i : i + 1, :] = row
    ga_send[15:16, :] = jnp.zeros((1, load), F32)
    moves = [
        send(ga_send, ga_recv.at[i], ga_ss.at[i], ga_rs.at[i], p, f) for i, p in enumerate(group)
    ]
    acc = ga_send[...]
    for i, m in enumerate(moves):
        m.wait_recv()
        acc = acc + ga_recv[i]
    gb_send[...] = acc
    moves = [
        send(gb_send, gb_recv.at[i], gb_ss.at[i], gb_rs.at[i], p, f) for i, p in enumerate(layers)
    ]
    for i, m in enumerate(moves):
        m.wait_recv()
        acc = acc + gb_recv[i]
    row = [acc[i : i + 1, :] for i in range(15)]
    weights = combination((
        (row[0], row[1]), row[2], (row[3], row[4]), (row[5], row[6]), row[7],
        (row[8], row[9]), (row[10], row[11]), (row[12], row[13]), row[14],
    ))
    basis = (v0, v1, u1, v2)

    def solved(start):
        rows = pl.ds(pl.multiple_of(start, CH), CH)
        re = im = None
        for (wr, wi), v in zip(weights, basis):
            a, b = v[rows, :load], v[rows, load:]
            tr, ti = wr * a - wi * b, wr * b + wi * a
            re, im = (tr, ti) if re is None else (re + tr, im + ti)
        return re, im

    def place(half, zt, yt_):
        if half == 0:
            return yt_ * (4 * CH) + (((zt + 1) // 2) % 2) * CH
        return yt_ * (4 * CH) + 2 * CH + (zt // 2) * CH

    z_moves, y_moves = [[], []], [[], []]
    for off in range(NY):
        for h in range(2):
            re, im = solved(place(h, za[h], yt(off)))
            z1s[h, off, :, :load] = re.astype(BF16)
            z1s[h, off, :, load:] = im.astype(BF16)
            z_moves[h].append(
                send(z1s.at[h, off], z1r.at[h, off], z1_ss.at[h, off], z1_rs.at[h, off], s, za[h] * NY + yt(off))
            )
    for off in range(1, NY):
        for h in range(2):
            re, im = solved(place(h, z, yt(off)))
            y1s[h, off - 1, :, :load] = re
            y1s[h, off - 1, :, load:] = im
            y_moves[h].append(
                send(y1s.at[h, off - 1], y1r.at[h, off - 1], y1_ss.at[h, off - 1], y1_rs.at[h, off - 1], s, z * NY + yt(off))
            )
    for h in range(2):
        re, im = solved(place(h, z, y))
        own[h, :, :load] = re
        own[h, :, load:] = im
    c_tbl.wait()

    def sources(h):
        out = [(z * NY + y, own.at[h])]
        out += [(z * NY + yf(off), y1r.at[h, off - 1]) for off in range(1, NY)]
        out += [(za[h] * NY + yf(off), z1r.at[h, off]) for off in range(NY)]
        return out

    def combine(h, zt):
        acc = [None] * NY
        for fs, ref in sources(h):
            re, im = ref[:, :load].astype(F32), ref[:, load:].astype(F32)
            for off in range(NY):
                at = ((zt * NY + yt(off)) * (4 * NY) + fs) * 2
                term = tbl[at] * re + tbl[at + 1] * im
                acc[off] = term if acc[off] is None else acc[off] + term
        return acc

    p_moves = [[], []]
    for h in range(2):
        for m in z_moves[h] + y_moves[h]:
            m.wait_recv()
        for slot, zt in enumerate((za[1 - h], opp)):
            acc = combine(h, zt)
            for off in range(NY):
                p2s[h, slot, off] = acc[off].astype(BF16)
            p_moves[h].append(
                send(p2s.at[h, slot], p2r.at[h, slot], p2_ss.at[h, slot], p2_rs.at[h, slot], s, za[1 - h] * NY + y)
            )
    for h in range(2):
        for slot, zt in ((1, za[h]), (0, z)):
            acc = combine(h, zt)
            for off in range(NY):
                keep[h, slot, off] = acc[off]

    z_moves, y_moves = [[], []], [[], []]
    for h in range(2):
        p_moves[h][1].wait_recv()
        for off in range(NY):
            z3s[h, off] = (keep[h, 1, off] + p2r[h, 1, off].astype(F32)).astype(BF16)
            z_moves[h].append(
                send(z3s.at[h, off], z3r.at[h, off], z3_ss.at[h, off], z3_rs.at[h, off], s, za[h] * NY + yt(off))
            )
    for h in range(2):
        p_moves[h][0].wait_recv()
        for off in range(1, NY):
            y3s[h, off - 1] = keep[h, 0, off] + p2r[h, 0, off].astype(F32)
            y_moves[h].append(
                send(y3s.at[h, off - 1], y3r.at[h, off - 1], y3_ss.at[h, off - 1], y3_rs.at[h, off - 1], s, z * NY + yt(off))
            )
        rows = pl.ds(pl.multiple_of(place(h, z, y), CH), CH)
        out_ref[rows, :] = keep[h, 0, 0] + p2r[h, 0, 0].astype(F32)
    for h in range(2):
        for off in range(1, NY):
            y_moves[h][off - 1].wait_recv()
            rows = pl.ds(pl.multiple_of(place(h, z, yf(off)), CH), CH)
            out_ref[rows, :] = y3r[h, off - 1]
    for h in range(2):
        for off in range(NY):
            z_moves[h][off].wait_recv()
            rows = pl.ds(pl.multiple_of(place(h, za[h], yf(off)), CH), CH)
            out_ref[rows, :] = z3r[h, off].astype(F32)
    for m in sends:
        m.wait_send()


def shards(right_side, schur, match_blocks):
    ni, _, _, loads = right_side.shape
    freqs = lax.axis_size("freq")
    wide = 2 * loads
    dma = pltpu.SemaphoreType.DMA
    vmem = pltpu.VMEM
    out = pl.pallas_call(
        kernel,
        out_shape=jax.ShapeDtypeStruct((ni, loads), F32),
        in_specs=[pl.BlockSpec(memory_space=pl.ANY)] * 4,
        out_specs=pl.BlockSpec(memory_space=pltpu.VMEM),
        scratch_shapes=[
            pltpu.SMEM((1, ROUNDS), jnp.int32),
            pltpu.SMEM((2 * freqs * freqs,), F32),
            vmem((2 * ni, loads), F32),
            vmem((2 * ni, ni), BF16),
            vmem((ni, wide), F32),
            vmem((ni, wide), F32),
            vmem((ni, wide), F32),
            vmem((ni, wide), F32),
            vmem((ni, wide), BF16),
            vmem((ni, wide), BF16),
            vmem((2 * ni, wide), F32),
            vmem((3, ROUNDS, BLOCK, wide), BF16),
            vmem((3, ROUNDS, BLOCK, wide), BF16),
            vmem((16, loads), F32),
            vmem((7, 16, loads), F32),
            vmem((16, loads), F32),
            vmem((3, 16, loads), F32),
            vmem((2, NY, CH, wide), BF16),
            vmem((2, NY, CH, wide), BF16),
            vmem((2, NY - 1, CH, wide), F32),
            vmem((2, NY - 1, CH, wide), F32),
            vmem((2, CH, wide), F32),
            vmem((2, 2, NY, CH, loads), BF16),
            vmem((2, 2, NY, CH, loads), BF16),
            vmem((2, 2, NY, CH, loads), F32),
            vmem((2, NY, CH, loads), BF16),
            vmem((2, NY, CH, loads), BF16),
            vmem((2, NY - 1, CH, loads), F32),
            vmem((2, NY - 1, CH, loads), F32),
            dma((4,)),
            dma((3, ROUNDS)), dma((3, ROUNDS)),
            dma((7,)), dma((7,)),
            dma((3,)), dma((3,)),
            dma((2, NY)), dma((2, NY)),
            dma((2, NY - 1)), dma((2, NY - 1)),
            dma((2, 2)), dma((2, 2)),
            dma((2, NY)), dma((2, NY)),
            dma((2, NY - 1)), dma((2, NY - 1)),
        ],
        compiler_params=pltpu.CompilerParams(
            collective_id=0, has_side_effects=True, vmem_limit_bytes=32 * 1024 * 1024
        ),
    )(
        match_blocks,
        jnp.asarray(phase_table(freqs)),
        right_side.reshape(2 * ni, loads),
        schur.reshape(2 * ni, ni),
    )
    return out.reshape(1, ni, loads)


def solution(mesh):
    return jax.shard_map(
        shards,
        mesh=mesh,
        in_specs=(P("sub", "freq", None, None), P("freq", None, "sub", None), P("sub", None)),
        out_specs=P("freq", "sub", None),
        check_vma=False,
    )
```

time: 424 us -> 64.9 us (0.15)
  blocking collectives: 203 us -> 0 us
  waiting for transfers between devices: 164 us -> 0 us
  Pallas kernels: 0 us -> 61 us
  starting transfers between devices: 26.9 us -> 0 us
  between operations: 15.8 us -> 0.01 us
  matrix products: 4.94 us -> 0 us
    psum x3 -> x0, blocking collectives: 203 us -> none  [shards(): num_re, num_im, den = lax.psum((part_re, part_im, part_den), 'sub')]
    reduce_scatter x1 -> x0, waiting for transfers between devices: 157 us -> none  [shards(): lax.psum_scatter(jnp.einsum('kfc,ifcl->kil', table, solution, precision=h...]
    pallas_call x0 -> x1, Pallas kernels: none -> 61 us  [shards(): pl.pallas_call(kernel, out_shape=jax.ShapeDtypeStruct((ni, loads), F32),...]
    ppermute x9 -> x0, starting transfers between devices: 26.9 us -> none  [partner(): return lax.ppermute(block, axis, route)]
    ppermute x9 -> x0, waiting for transfers between devices: 6.13 us -> none  [partner(): return lax.ppermute(block, axis, route)]
    dot_general x4 -> x0, matrix products: 4.94 us -> none  [the longest x1 3.55 us: shards(): jnp.einsum('kfc,ifcl->kil', table, solution, precision=high)]
  transfers between devices with their start and end apart: 10 -> 0, of which waited for: 4 -> 0; matrix products, arithmetic and copies ran while one was open for 1% -> 0% of each run, Pallas kernels for 0% -> 0%
where the time goes in v1:
time: 64.9 us; the launch traced here: 64.7 us
  Pallas kernels  61 us (94%)
  local copies, waits for them, and re-layouts  3.65 us (6%)
    pallas_call x1, Pallas kernels, shards(): pl.pallas_call(kernel, out_shape=jax.ShapeDtypeStruct((ni, loads), F32),...  61 us
    unnamed x9, local copies, waits for them, and re-layouts  3.65 us

profile of v1, /device:TPU:1, one launch (start us, length us, event | category | flops | bytes accessed | tf_op | source)
XLA Modules:
  0.0 64.7 jit_solution(14487921040899999356)
XLA Ops:
  0.0 0.0 copy-start.2
  0.0 0.0 copy-start.3
  0.0 0.7 %copy-done.2 = f32[512]{0:T(512)S(1)} copy-done((f32[512]{0:T(512)S(1)}, f32[512]{0:T(512)}, u32[]{:S(2)}) %copy-start.2) | copy-done | bytes 2072
  0.7 0.0 copy-done.3
  0.7 0.0 copy-start
  0.7 1.2 %copy-done = bf16[1,2,512,512]{3,2,1,0:T(8,128)(2,1)S(1)} copy-done((bf16[1,2,512,512]{3,2,1,0:T(8,128)(2,1)S(1)}, bf16[1,2,512,512]{3,2,1,0:T(8,128)(2,1)}, u32[]{:S(2)}) %copy-start) | copy-done | bytes 1048600
  1.9 0.0 copy-start.1
  1.9 1.0 %copy-done.1 = f32[512,1,2,128]{3,2,1,0:T(2,128)S(1)} copy-done((f32[512,1,2,128]{3,2,1,0:T(2,128)S(1)}, f32[512,1,2,128]{3,2,1,0:T(2,128)}, u32[]{:S(2)}) %copy-start.1) | copy-done | bytes 524312
  3.0 61.0 %shard_map.46 = f32[512,128]{1,0:T(8,128)S(1)} custom-call(s32[1,3]{1,0:T(1,128)S(1)} %copy-done.3, f32[512]{0:T(512)S(1)} %copy-done.2, f32[1024,128]{1,0:T(8,128)S(1)} %bitcast.5, bf16[1024,512]{1,0:T(8,128)(2,1)S(1)} %bitcast.3), custom_call_target="tpu_custom_call" | custom-call | tf_op jit(solution)/shard_map/pallas_call | solution.py:389
  64.0 0.7 %copy.6 = f32[1,512,128]{2,1,0:T(8,128)} copy(f32[1,512,128]{2,1,0:T(8,128)S(1)} %bitcast.4) | data formatting | bytes 524288
Async XLA Ops:
  0.0 0.7 %copy-start.2 = (f32[512]{0:T(512)S(1)}, f32[512]{0:T(512)}, u32[]{:S(2)}) copy-start(f32[512]{0:T(512)} %constant.2.clone.tbl_hbm) | copy-start | bytes 6148
  0.0 0.7 %copy-start.3 = (s32[1,3]{1,0:T(1,128)S(1)}, s32[1,3]{1,0:T(1,128)}, u32[]{:S(2)}) copy-start(s32[1,3]{1,0:T(1,128)} %mb_hbm.1) | copy-start | bytes 40
  0.7 1.2 %copy-start = (bf16[1,2,512,512]{3,2,1,0:T(8,128)(2,1)S(1)}, bf16[1,2,512,512]{3,2,1,0:T(8,128)(2,1)}, u32[]{:S(2)}) copy-start(bf16[1,2,512,512]{3,2,1,0:T(8,128)(2,1)} %param.5) | copy-start | bytes 3145732
  1.9 1.0 %copy-start.1 = (f32[512,1,2,128]{3,2,1,0:T(2,128)S(1)}, f32[512,1,2,128]{3,2,1,0:T(2,128)}, u32[]{:S(2)}) copy-start(f32[512,1,2,128]{3,2,1,0:T(2,128)} %param.4) | copy-start | bytes 1572868

commit v2 on v1

--- a/solution.py
+++ b/solution.py
@@ -389,7 +389,7 @@
     out = pl.pallas_call(
         kernel,
         out_shape=jax.ShapeDtypeStruct((ni, loads), F32),
-        in_specs=[pl.BlockSpec(memory_space=pl.ANY)] * 4,
+        in_specs=[pl.BlockSpec(memory_space=pltpu.HBM)] * 4,
         out_specs=pl.BlockSpec(memory_space=pltpu.VMEM),
         scratch_shapes=[
             pltpu.SMEM((1, ROUNDS), jnp.int32),
@@ -432,7 +432,7 @@
             dma((2, NY - 1)), dma((2, NY - 1)),
         ],
         compiler_params=pltpu.CompilerParams(
-            collective_id=0, has_side_effects=True, vmem_limit_bytes=32 * 1024 * 1024
+            collective_id=0, has_side_effects=True, vmem_limit_bytes=60 * 1024 * 1024
         ),
     )(
         match_blocks,

time: 64.9 us -> 63.5 us (0.978)
  local copies, waits for them, and re-layouts: 3.65 us -> 1.67 us
    unnamed x9 -> x1, local copies, waits for them, and re-layouts: 3.65 us -> 1.67 us
where the time goes in v2:
time: 63.5 us; the launch traced here: 63.3 us
  Pallas kernels  61.6 us (97%)
  local copies, waits for them, and re-layouts  1.67 us (3%)
    pallas_call x1, Pallas kernels, shards(): pl.pallas_call(kernel, out_shape=jax.ShapeDtypeStruct((ni, loads), F32),...  61.6 us
    unnamed x1, local copies, waits for them, and re-layouts  1.67 us

profile of v2, /device:TPU:1, one launch (start us, length us, event | category | flops | bytes accessed | tf_op | source)
XLA Modules:
  0.0 63.3 jit_solution(13694382525534362455)
XLA Ops:
  0.0 61.6 %shard_map.46 = f32[512,128]{1,0:T(8,128)} custom-call(s32[1,3]{1,0:T(1,128)} %mb_hbm.1, f32[512]{0:T(512)} %constant.2.clone.tbl_hbm, f32[1024,128]{1,0:T(8,128)} %bitcast.5, bf16[1024,512]{1,0:T(8,128)(2,1)} %bitcast.3), custom_call_target="tpu_custom_call" | custom-call | tf_op jit(solution)/shard_map/pallas_call | solution.py:389
  61.6 1.7 %copy.6 = f32[1,512,128]{2,1,0:T(8,128)} copy(f32[1,512,128]{2,1,0:T(8,128)} %bitcast.4) | data formatting | bytes 524288

commit v3 on v2

--- a/solution.py
+++ b/solution.py
@@ -17,6 +17,8 @@
 ROUNDS = 3
 NY = 4
 CH = 32
+PARTS = 1
+PIECE = CH // PARTS
 
 
 def phase_table(count):
@@ -129,29 +131,30 @@
 
     c_mb = pltpu.make_async_copy(mb_hbm, mb, in_sem.at[0])
     c_tbl = pltpu.make_async_copy(tbl_hbm, tbl, in_sem.at[1])
-    c_rs = pltpu.make_async_copy(rs_hbm, rs, in_sem.at[2])
-    c_sch = pltpu.make_async_copy(sch_hbm, sch, in_sem.at[3])
-    c_rs.start()
-    c_mb.start()
-    c_sch.start()
-    c_tbl.start()
+    c_sch = pltpu.make_async_copy(sch_hbm, sch, in_sem.at[2])
+    c_rs = []
+    for k in range(nb):
+        rows = pl.ds(2 * BLOCK * k, 2 * BLOCK)
+        c_rs.append(pltpu.make_async_copy(rs_hbm.at[rows], rs.at[rows], in_sem.at[3 + k]))
+    for copy in c_rs + [c_mb, c_sch, c_tbl]:
+        copy.start()
 
     barrier = pltpu.get_barrier_semaphore()
-    peers = [(p, f) for p in group + layers]
+    peers = [(s, zt * NY + yt(off)) for off in (2, 1, 3, 0) for zt in za]
+    peers += [(p, f) for p in layers[::-1] + group]
     peers += [(s, z * NY + yt(off)) for off in range(1, NY)]
-    peers += [(s, zt * NY + yt(off)) for zt in za for off in range(NY)]
     for ps, pf in peers:
         pl.semaphore_signal(barrier, inc=1, device_id={"sub": ps, "freq": pf}, device_id_type=MESH)
 
-    c_rs.wait()
-    for k in range(nb):
+    def halves_of(k):
         for c in range(2):
             part = rs[pl.ds(2 * BLOCK * k + c, BLOCK, stride=2), :]
-            rows, cols = pl.ds(k * BLOCK, BLOCK), pl.ds(c * load, load)
-            v0[rows, cols] = part
-            high = part.astype(BF16)
-            q[rows, cols] = high
-            qlo[rows, cols] = (part - high.astype(F32)).astype(BF16)
+            yield part, pl.ds(k * BLOCK, BLOCK), pl.ds(c * load, load)
+
+    for k in range(nb):
+        c_rs[k].wait()
+        for part, rows, cols in halves_of(k):
+            q[rows, cols] = part.astype(BF16)
     c_mb.wait()
     pl.semaphore_wait(barrier, len(peers))
 
@@ -200,6 +203,10 @@
         return [jnp.sum(a, axis=0, keepdims=True) for a in acc]
 
     moves = exchange(0)
+    for k in range(nb):
+        for part, rows, cols in halves_of(k):
+            v0[rows, cols] = part
+            qlo[rows, cols] = (part - q[rows, cols].astype(F32)).astype(BF16)
     c_sch.wait()
     prod[...] = jnp.dot(sch[...], qlo[...], preferred_element_type=F32)
     for k in range(nb):
@@ -280,7 +287,7 @@
     basis = (v0, v1, u1, v2)
 
     def solved(start):
-        rows = pl.ds(pl.multiple_of(start, CH), CH)
+        rows = pl.ds(pl.multiple_of(start, PIECE), PIECE)
         re = im = None
         for (wr, wi), v in zip(weights, basis):
             a, b = v[rows, :load], v[rows, load:]
@@ -288,94 +295,109 @@
             re, im = (tr, ti) if re is None else (re + tr, im + ti)
         return re, im
 
-    def place(half, zt, yt_):
+    def place(c, half, zt, yt_):
+        first = yt_ * (4 * CH) + c * PIECE
         if half == 0:
-            return yt_ * (4 * CH) + (((zt + 1) // 2) % 2) * CH
-        return yt_ * (4 * CH) + 2 * CH + (zt // 2) * CH
-
-    z_moves, y_moves = [[], []], [[], []]
-    for off in range(NY):
-        for h in range(2):
-            re, im = solved(place(h, za[h], yt(off)))
-            z1s[h, off, :, :load] = re.astype(BF16)
-            z1s[h, off, :, load:] = im.astype(BF16)
-            z_moves[h].append(
-                send(z1s.at[h, off], z1r.at[h, off], z1_ss.at[h, off], z1_rs.at[h, off], s, za[h] * NY + yt(off))
-            )
-    for off in range(1, NY):
-        for h in range(2):
-            re, im = solved(place(h, z, yt(off)))
-            y1s[h, off - 1, :, :load] = re
-            y1s[h, off - 1, :, load:] = im
-            y_moves[h].append(
-                send(y1s.at[h, off - 1], y1r.at[h, off - 1], y1_ss.at[h, off - 1], y1_rs.at[h, off - 1], s, z * NY + yt(off))
-            )
-    for h in range(2):
-        re, im = solved(place(h, z, y))
-        own[h, :, :load] = re
-        own[h, :, load:] = im
+            return first + (((zt + 1) // 2) % 2) * CH
+        return first + 2 * CH + (zt // 2) * CH
+
+    parts, halves, offs = range(PARTS), range(2), range(NY)
+
+    z_moves, y_moves = {}, {}
+    for c in parts:
+        for off in (2, 1, 3, 0):
+            for h in halves:
+                re, im = solved(place(c, h, za[h], yt(off)))
+                z1s[c, h, off, :, :load] = re.astype(BF16)
+                z1s[c, h, off, :, load:] = im.astype(BF16)
+                z_moves[c, h, off] = send(
+                    z1s.at[c, h, off], z1r.at[c, h, off], z1_ss.at[c, h, off], z1_rs.at[c, h, off],
+                    s, za[h] * NY + yt(off),
+                )
+        for off in (2, 1, 3):
+            for h in halves:
+                re, im = solved(place(c, h, z, yt(off)))
+                y1s[c, h, off - 1, :, :load] = re
+                y1s[c, h, off - 1, :, load:] = im
+                y_moves[c, h, off] = send(
+                    y1s.at[c, h, off - 1], y1r.at[c, h, off - 1], y1_ss.at[c, h, off - 1], y1_rs.at[c, h, off - 1],
+                    s, z * NY + yt(off),
+                )
+    for c in parts:
+        for h in halves:
+            re, im = solved(place(c, h, z, y))
+            own[c, h, :, :load] = re
+            own[c, h, :, load:] = im
     c_tbl.wait()
 
-    def sources(h):
-        out = [(z * NY + y, own.at[h])]
-        out += [(z * NY + yf(off), y1r.at[h, off - 1]) for off in range(1, NY)]
-        out += [(za[h] * NY + yf(off), z1r.at[h, off]) for off in range(NY)]
+    def sources(c, h):
+        out = [(z * NY + y, own.at[c, h])]
+        out += [(z * NY + yf(off), y1r.at[c, h, off - 1]) for off in offs[1:]]
+        out += [(za[h] * NY + yf(off), z1r.at[c, h, off]) for off in offs]
         return out
 
-    def combine(h, zt):
+    def combine(c, h, zt):
         acc = [None] * NY
-        for fs, ref in sources(h):
+        for fs, ref in sources(c, h):
             re, im = ref[:, :load].astype(F32), ref[:, load:].astype(F32)
-            for off in range(NY):
+            for off in offs:
                 at = ((zt * NY + yt(off)) * (4 * NY) + fs) * 2
                 term = tbl[at] * re + tbl[at + 1] * im
                 acc[off] = term if acc[off] is None else acc[off] + term
         return acc
 
-    p_moves = [[], []]
-    for h in range(2):
-        for m in z_moves[h] + y_moves[h]:
-            m.wait_recv()
-        for slot, zt in enumerate((za[1 - h], opp)):
-            acc = combine(h, zt)
-            for off in range(NY):
-                p2s[h, slot, off] = acc[off].astype(BF16)
-            p_moves[h].append(
-                send(p2s.at[h, slot], p2r.at[h, slot], p2_ss.at[h, slot], p2_rs.at[h, slot], s, za[1 - h] * NY + y)
-            )
-    for h in range(2):
-        for slot, zt in ((1, za[h]), (0, z)):
-            acc = combine(h, zt)
-            for off in range(NY):
-                keep[h, slot, off] = acc[off]
-
-    z_moves, y_moves = [[], []], [[], []]
-    for h in range(2):
-        p_moves[h][1].wait_recv()
-        for off in range(NY):
-            z3s[h, off] = (keep[h, 1, off] + p2r[h, 1, off].astype(F32)).astype(BF16)
-            z_moves[h].append(
-                send(z3s.at[h, off], z3r.at[h, off], z3_ss.at[h, off], z3_rs.at[h, off], s, za[h] * NY + yt(off))
-            )
-    for h in range(2):
-        p_moves[h][0].wait_recv()
-        for off in range(1, NY):
-            y3s[h, off - 1] = keep[h, 0, off] + p2r[h, 0, off].astype(F32)
-            y_moves[h].append(
-                send(y3s.at[h, off - 1], y3r.at[h, off - 1], y3_ss.at[h, off - 1], y3_rs.at[h, off - 1], s, z * NY + yt(off))
-            )
-        rows = pl.ds(pl.multiple_of(place(h, z, y), CH), CH)
-        out_ref[rows, :] = keep[h, 0, 0] + p2r[h, 0, 0].astype(F32)
-    for h in range(2):
-        for off in range(1, NY):
-            y_moves[h][off - 1].wait_recv()
-            rows = pl.ds(pl.multiple_of(place(h, z, yf(off)), CH), CH)
-            out_ref[rows, :] = y3r[h, off - 1]
-    for h in range(2):
-        for off in range(NY):
-            z_moves[h][off].wait_recv()
-            rows = pl.ds(pl.multiple_of(place(h, za[h], yf(off)), CH), CH)
-            out_ref[rows, :] = z3r[h, off].astype(F32)
+    p_moves = {}
+    for c in parts:
+        for h in halves:
+            for off in offs[1:]:
+                y_moves[c, h, off].wait_recv()
+            for off in offs:
+                z_moves[c, h, off].wait_recv()
+            for slot, zt in ((1, opp), (0, za[1 - h])):
+                acc = combine(c, h, zt)
+                for off in offs:
+                    p2s[c, h, slot, off] = acc[off].astype(BF16)
+                p_moves[c, h, slot] = send(
+                    p2s.at[c, h, slot], p2r.at[c, h, slot], p2_ss.at[c, h, slot], p2_rs.at[c, h, slot],
+                    s, za[1 - h] * NY + y,
+                )
+        for h in halves:
+            for slot, zt in ((1, za[h]), (0, z)):
+                acc = combine(c, h, zt)
+                for off in offs:
+                    keep[c, h, slot, off] = acc[off]
+
+    z_moves, y_moves = {}, {}
+    for c in parts:
+        for h in halves:
+            p_moves[c, h, 1].wait_recv()
+            for off in (2, 1, 3, 0):
+                z3s[c, h, off] = (keep[c, h, 1, off] + p2r[c, h, 1, off].astype(F32)).astype(BF16)
+                z_moves[c, h, off] = send(
+                    z3s.at[c, h, off], z3r.at[c, h, off], z3_ss.at[c, h, off], z3_rs.at[c, h, off],
+                    s, za[h] * NY + yt(off),
+                )
+        for h in halves:
+            p_moves[c, h, 0].wait_recv()
+            for off in (2, 1, 3):
+                y3s[c, h, off - 1] = keep[c, h, 0, off] + p2r[c, h, 0, off].astype(F32)
+                y_moves[c, h, off] = send(
+                    y3s.at[c, h, off - 1], y3r.at[c, h, off - 1], y3_ss.at[c, h, off - 1], y3_rs.at[c, h, off - 1],
+                    s, z * NY + yt(off),
+                )
+            rows = pl.ds(pl.multiple_of(place(c, h, z, y), PIECE), PIECE)
+            out_ref[rows, :] = keep[c, h, 0, 0] + p2r[c, h, 0, 0].astype(F32)
+    for c in parts:
+        for h in halves:
+            for off in offs[1:]:
+                y_moves[c, h, off].wait_recv()
+                rows = pl.ds(pl.multiple_of(place(c, h, z, yf(off)), PIECE), PIECE)
+                out_ref[rows, :] = y3r[c, h, off - 1]
+        for h in halves:
+            for off in offs:
+                z_moves[c, h, off].wait_recv()
+                rows = pl.ds(pl.multiple_of(place(c, h, za[h], yf(off)), PIECE), PIECE)
+                out_ref[rows, :] = z3r[c, h, off].astype(F32)
     for m in sends:
         m.wait_send()
 
@@ -388,7 +410,7 @@
     vmem = pltpu.VMEM
     out = pl.pallas_call(
         kernel,
-        out_shape=jax.ShapeDtypeStruct((ni, loads), F32),
+        out_shape=pltpu.VMEM((ni, loads), F32),
         in_specs=[pl.BlockSpec(memory_space=pltpu.HBM)] * 4,
         out_specs=pl.BlockSpec(memory_space=pltpu.VMEM),
         scratch_shapes=[
@@ -409,27 +431,27 @@
             vmem((7, 16, loads), F32),
             vmem((16, loads), F32),
             vmem((3, 16, loads), F32),
-            vmem((2, NY, CH, wide), BF16),
-            vmem((2, NY, CH, wide), BF16),
-            vmem((2, NY - 1, CH, wide), F32),
-            vmem((2, NY - 1, CH, wide), F32),
-            vmem((2, CH, wide), F32),
-            vmem((2, 2, NY, CH, loads), BF16),
-            vmem((2, 2, NY, CH, loads), BF16),
-            vmem((2, 2, NY, CH, loads), F32),
-            vmem((2, NY, CH, loads), BF16),
-            vmem((2, NY, CH, loads), BF16),
-            vmem((2, NY - 1, CH, loads), F32),
-            vmem((2, NY - 1, CH, loads), F32),
-            dma((4,)),
+            vmem((PARTS, 2, NY, PIECE, wide), BF16),
+            vmem((PARTS, 2, NY, PIECE, wide), BF16),
+            vmem((PARTS, 2, NY - 1, PIECE, wide), F32),
+            vmem((PARTS, 2, NY - 1, PIECE, wide), F32),
+            vmem((PARTS, 2, PIECE, wide), F32),
+            vmem((PARTS, 2, 2, NY, PIECE, loads), BF16),
+            vmem((PARTS, 2, 2, NY, PIECE, loads), BF16),
+            vmem((PARTS, 2, 2, NY, PIECE, loads), F32),
+            vmem((PARTS, 2, NY, PIECE, loads), BF16),
+            vmem((PARTS, 2, NY, PIECE, loads), BF16),
+            vmem((PARTS, 2, NY - 1, PIECE, loads), F32),
+            vmem((PARTS, 2, NY - 1, PIECE, loads), F32),
+            dma((3 + ni // BLOCK,)),
             dma((3, ROUNDS)), dma((3, ROUNDS)),
             dma((7,)), dma((7,)),
             dma((3,)), dma((3,)),
-            dma((2, NY)), dma((2, NY)),
-            dma((2, NY - 1)), dma((2, NY - 1)),
-            dma((2, 2)), dma((2, 2)),
-            dma((2, NY)), dma((2, NY)),
-            dma((2, NY - 1)), dma((2, NY - 1)),
+            dma((PARTS, 2, NY)), dma((PARTS, 2, NY)),
+            dma((PARTS, 2, NY - 1)), dma((PARTS, 2, NY - 1)),
+            dma((PARTS, 2, 2)), dma((PARTS, 2, 2)),
+            dma((PARTS, 2, NY)), dma((PARTS, 2, NY)),
+            dma((PARTS, 2, NY - 1)), dma((PARTS, 2, NY - 1)),
         ],
         compiler_params=pltpu.CompilerParams(
             collective_id=0, has_side_effects=True, vmem_limit_bytes=60 * 1024 * 1024

time: 63.5 us -> 58.7 us (0.924)
  Pallas kernels: 61.6 us -> 57.9 us
  local copies, waits for them, and re-layouts: 1.67 us -> 0.71 us
    pallas_call x1, Pallas kernels: 61.6 us -> 57.9 us  [shards(): pl.pallas_call(kernel, out_shape=pltpu.VMEM((ni, loads), F32), in_specs=[...]
    unnamed x1, local copies, waits for them, and re-layouts: 1.67 us -> 0.71 us
where the time goes in v3:
time: 58.7 us; the launch traced here: 58.6 us
  Pallas kernels  57.9 us (99%)
  local copies, waits for them, and re-layouts  0.71 us (1%)
    pallas_call x1, Pallas kernels, shards(): pl.pallas_call(kernel, out_shape=pltpu.VMEM((ni, loads), F32), in_specs=[...  57.9 us

profile of v3, /device:TPU:1, one launch (start us, length us, event | category | flops | bytes accessed | tf_op | source)
XLA Modules:
  0.0 58.6 jit_solution(1986161617040303183)
XLA Ops:
  0.0 57.9 %shard_map.46 = f32[512,128]{1,0:T(8,128)S(1)} custom-call(s32[1,3]{1,0:T(1,128)} %mb_hbm.1, f32[512]{0:T(512)} %constant.2.clone.tbl_hbm, f32[1024,128]{1,0:T(8,128)} %bitcast.5, bf16[1024,512]{1,0:T(8,128)(2,1)} %bitcast.4), custom_call_target="tpu_custom_call" | custom-call | tf_op jit(solution)/shard_map/pallas_call | solution.py:411
  57.9 0.7 %copy.6 = f32[1,512,128]{2,1,0:T(8,128)} copy(f32[1,512,128]{2,1,0:T(8,128)S(1)} %bitcast.3) | data formatting | bytes 524288

commit v4 on v3

--- a/solution.py
+++ b/solution.py
@@ -17,7 +17,7 @@
 ROUNDS = 3
 NY = 4
 CH = 32
-PARTS = 1
+PARTS = 2
 PIECE = CH // PARTS
 
 
@@ -105,7 +105,7 @@
         return s + bit - 2 * bit * ((s // bit) % 2)
 
     partners = [flip(1), flip(2), flip(8)]
-    group = [(s // 8) * 8 + (s + off) % 8 for off in range(1, 8)]
+    group = [(s // 8) * 8 + (s + off) % 8 for off in (7, 6, 5, 4, 3, 2, 1)]
     layers = [(s + 8 * off) % nsub for off in range(1, 4)]
     ze = z + 1 - 2 * (z % 2)
     zo = 3 - z
@@ -119,6 +119,12 @@
         return (y + NY - off) % NY
 
     sends = []
+
+    def left(copies):
+        for m in copies:
+            m.wait_send()
+        sends[:] = [m for m in sends if all(m is not o for o in copies)]
+
 
     def send(src, dst, ss, rsem, sub, freq):
         copy = pltpu.make_async_remote_copy(
@@ -305,6 +311,8 @@
 
     z_moves, y_moves = {}, {}
     for c in parts:
+        if c:
+            left([z_moves[c - 1, h, off] for h in halves for off in offs])
         for off in (2, 1, 3, 0):
             for h in halves:
                 re, im = solved(place(c, h, za[h], yt(off)))
@@ -347,25 +355,36 @@
         return acc
 
     p_moves = {}
+
+    def pass_on(c, h, slot):
+        acc = combine(c, h, opp if slot else za[1 - h])
+        for off in offs:
+            p2s[c, h, slot, off] = acc[off].astype(BF16)
+        p_moves[c, h, slot] = send(
+            p2s.at[c, h, slot], p2r.at[c, h, slot], p2_ss.at[c, h, slot], p2_rs.at[c, h, slot],
+            s, za[1 - h] * NY + y,
+        )
+
+    def hold(c, h, slot):
+        acc = combine(c, h, za[h] if slot else z)
+        for off in offs:
+            keep[c, h, slot, off] = acc[off]
+
     for c in parts:
         for h in halves:
             for off in offs[1:]:
                 y_moves[c, h, off].wait_recv()
             for off in offs:
                 z_moves[c, h, off].wait_recv()
-            for slot, zt in ((1, opp), (0, za[1 - h])):
-                acc = combine(c, h, zt)
-                for off in offs:
-                    p2s[c, h, slot, off] = acc[off].astype(BF16)
-                p_moves[c, h, slot] = send(
-                    p2s.at[c, h, slot], p2r.at[c, h, slot], p2_ss.at[c, h, slot], p2_rs.at[c, h, slot],
-                    s, za[1 - h] * NY + y,
-                )
-        for h in halves:
-            for slot, zt in ((1, za[h]), (0, z)):
-                acc = combine(c, h, zt)
-                for off in offs:
-                    keep[c, h, slot, off] = acc[off]
+            pass_on(c, h, 1)
+    left([p_moves[c, h, 1] for c in parts for h in halves])
+    for c in parts:
+        for h in halves:
+            pass_on(c, h, 0)
+    for slot in (1, 0):
+        for c in parts:
+            for h in halves:
+                hold(c, h, slot)
 
     z_moves, y_moves = {}, {}
     for c in parts:
@@ -377,6 +396,7 @@
                     z3s.at[c, h, off], z3r.at[c, h, off], z3_ss.at[c, h, off], z3_rs.at[c, h, off],
                     s, za[h] * NY + yt(off),
                 )
+    for c in parts:
         for h in halves:
             p_moves[c, h, 0].wait_recv()
             for off in (2, 1, 3):

time: 58.7 us -> 56.7 us (0.966)
  the two profiles are of different devices: /device:TPU:1 before, /device:TPU:2 now
where the time goes in v4:
time: 56.7 us; the launch traced here: 56.5 us
  Pallas kernels  55.8 us (98%)
  local copies, waits for them, and re-layouts  0.71 us (1%)
    pallas_call x1, Pallas kernels, shards(): pl.pallas_call(kernel, out_shape=pltpu.VMEM((ni, loads), F32), in_specs=[...  55.8 us

profile of v4, /device:TPU:2, one launch (start us, length us, event | category | flops | bytes accessed | tf_op | source)
XLA Modules:
  0.0 56.5 jit_solution(11651477962773093538)
XLA Ops:
  0.0 55.8 %shard_map.46 = f32[512,128]{1,0:T(8,128)S(1)} custom-call(s32[1,3]{1,0:T(1,128)} %mb_hbm.1, f32[512]{0:T(512)} %constant.2.clone.tbl_hbm, f32[1024,128]{1,0:T(8,128)} %bitcast.5, bf16[1024,512]{1,0:T(8,128)(2,1)} %bitcast.4), custom_call_target="tpu_custom_call" | custom-call | tf_op jit(solution)/shard_map/pallas_call | solution.py:431
  55.8 0.7 %copy.6 = f32[1,512,128]{2,1,0:T(8,128)} copy(f32[1,512,128]{2,1,0:T(8,128)S(1)} %bitcast.3) | data formatting | bytes 524288

commit v5 on v4

--- a/solution.py
+++ b/solution.py
@@ -322,6 +322,7 @@
                     z1s.at[c, h, off], z1r.at[c, h, off], z1_ss.at[c, h, off], z1_rs.at[c, h, off],
                     s, za[h] * NY + yt(off),
                 )
+    for c in parts:
         for off in (2, 1, 3):
             for h in halves:
                 re, im = solved(place(c, h, z, yt(off)))

time: 56.7 us -> 56.4 us (level)
  the two profiles are of different devices: /device:TPU:2 before, /device:TPU:1 now
where the time goes in v5:
time: 56.4 us; the launch traced here: 55.2 us
  Pallas kernels  54.5 us (97%)
  local copies, waits for them, and re-layouts  0.71 us (1%)
    pallas_call x1, Pallas kernels, shards(): pl.pallas_call(kernel, out_shape=pltpu.VMEM((ni, loads), F32), in_specs=[...  54.5 us

profile of v5, /device:TPU:1, one launch (start us, length us, event | category | flops | bytes accessed | tf_op | source)
XLA Modules:
  0.0 55.2 jit_solution(16941364035560621177)
XLA Ops:
  0.0 54.5 %shard_map.46 = f32[512,128]{1,0:T(8,128)S(1)} custom-call(s32[1,3]{1,0:T(1,128)} %mb_hbm.1, f32[512]{0:T(512)} %constant.2.clone.tbl_hbm, f32[1024,128]{1,0:T(8,128)} %bitcast.5, bf16[1024,512]{1,0:T(8,128)(2,1)} %bitcast.4), custom_call_target="tpu_custom_call" | custom-call | tf_op jit(solution)/shard_map/pallas_call | solution.py:432
  54.5 0.7 %copy.6 = f32[1,512,128]{2,1,0:T(8,128)} copy(f32[1,512,128]{2,1,0:T(8,128)S(1)} %bitcast.3) | data formatting | bytes 524288

commit v6 on v5

--- a/solution.py
+++ b/solution.py
@@ -380,6 +380,8 @@
             pass_on(c, h, 1)
     left([p_moves[c, h, 1] for c in parts for h in halves])
     for c in parts:
+        if c:
+            left([p_moves[c - 1, h, 0] for h in halves])
         for h in halves:
             pass_on(c, h, 0)
     for slot in (1, 0):

time: 56.4 us -> 56.8 us (level)
  the two profiles are of different devices: /device:TPU:1 before, /device:TPU:8 now
where the time goes in v6:
time: 56.8 us; the launch traced here: 56.7 us
  Pallas kernels  56 us (99%)
  local copies, waits for them, and re-layouts  0.71 us (1%)
    pallas_call x1, Pallas kernels, shards(): pl.pallas_call(kernel, out_shape=pltpu.VMEM((ni, loads), F32), in_specs=[...  56 us

profile of v6, /device:TPU:8, one launch (start us, length us, event | category | flops | bytes accessed | tf_op | source)
XLA Modules:
  0.0 56.7 jit_solution(13554899863208181665)
XLA Ops:
  0.0 56.0 %shard_map.46 = f32[512,128]{1,0:T(8,128)S(1)} custom-call(s32[1,3]{1,0:T(1,128)} %mb_hbm.1, f32[512]{0:T(512)} %constant.2.clone.tbl_hbm, f32[1024,128]{1,0:T(8,128)} %bitcast.5, bf16[1024,512]{1,0:T(8,128)(2,1)} %bitcast.4), custom_call_target="tpu_custom_call" | custom-call | tf_op jit(solution)/shard_map/pallas_call | solution.py:434
  56.0 0.7 %copy.6 = f32[1,512,128]{2,1,0:T(8,128)} copy(f32[1,512,128]{2,1,0:T(8,128)S(1)} %bitcast.3) | data formatting | bytes 524288
